TPU v7x, 256 devices: a whole 4x4x8 slice. The times are simulated.
256 devices in a mesh: seq: 64 (over y, z, core), chan: 4 (over x).
Axes of the slice: x: 4, y: 4, z: 8, core: 2. Of those that a mesh axis runs over, the one named last changes fastest.
Arguments:
- inputs: bfloat16 [32768, 1536], P('seq', 'chan'), may hold values from -16 to 16
- conv_weight: bfloat16 [1, 3, 1536, 1536], P(None, None, None, 'chan'), may hold values from -0.09375 to 0.09375
- head_weight: bfloat16 [1536, 4096], P(None, 'chan'), may hold values from -0.15625 to 0.15625
- head_cot: bfloat16 [32768, 4096], P('seq', 'chan'), may hold values from -6 to 6
- exon_blocks: int32 [512, 8], P('seq'), may hold values from 0 to 255
Outputs:
- tracks: bfloat16 [32768, 4096], P('seq', 'chan')
- coverage: float32 [512, 4096], P('seq', 'chan')
- input_grad: bfloat16 [32768, 1536], P('seq', 'chan')
- kernel_gradient: float32 [1, 3, 1536, 1536], P(None, None, 'seq', 'chan')
All inputs are finite; a program needn't handle non-finite values.
Results may differ from a plain program's by a relative error of at most 0.0059.
Values may be sent and summed in bfloat16 or wider, within the bound.
No kernel may reach another device: no remote copies, remote signals or barrier semaphores. Data moves between devices by JAX's collectives and lax.ppermute only.
A program may use at most 64 MiB of HBM per device.

v0:
```python
import jax
import jax.numpy as jnp
from jax import lax
from jax.sharding import PartitionSpec as P

BLOCK = 128
EXONS = 8


def shifted(value, axis, steps):
    count = lax.axis_size(axis)
    leading, last = (max(0, -steps), min(count, count - steps))
    return lax.ppermute(value, axis, [(source, source + steps) for source in range(leading, last)])


def activation_slope(point, cotan):
    _, back = jax.vjp(jax.nn.gelu, point)
    return back(cotan)[0]


def tap_input(values, steps):
    return shifted(values, "seq", steps)


def tap_grad(values, steps):
    return shifted(values, "seq", steps)


def times_t(left, right):
    return lax.dot_general(
        left, right, (((1,), (1,)), ((), ())), preferred_element_type=jnp.float32
    )


def inner_rows(left, right):
    return lax.dot_general(
        left, right, (((0,), (0,)), ((), ())), preferred_element_type=jnp.float32
    )


def shards(inputs, conv_weight, head_weight, head_cot, exon_blocks):
    rows = inputs.shape[0]
    state = inputs
    layer_number = 0
    steps = 2 * 2**layer_number
    acted = jax.nn.gelu(state.astype(jnp.float32)).astype(jnp.bfloat16)
    lower = tap_input(acted, steps)
    upper = tap_input(acted, -steps)
    whole = lax.all_gather(acted, "chan", axis=1, tiled=True)
    whole_low = lax.all_gather(lower, "chan", axis=1, tiled=True)
    whole_up = lax.all_gather(upper, "chan", axis=1, tiled=True)
    mixed = jnp.dot(whole_low, conv_weight[layer_number, 0], preferred_element_type=jnp.float32)
    mixed = mixed + jnp.dot(whole, conv_weight[layer_number, 1], preferred_element_type=jnp.float32)
    mixed = mixed + jnp.dot(
        whole_up, conv_weight[layer_number, 2], preferred_element_type=jnp.float32
    )
    saved = [(state, whole, steps)]
    state = (state.astype(jnp.float32) + mixed).astype(jnp.bfloat16)
    full_state = lax.all_gather(state, "chan", axis=1, tiled=True)
    logits = jnp.dot(full_state, head_weight, preferred_element_type=jnp.float32)
    tracks = jax.nn.softplus(logits).astype(jnp.bfloat16)
    head_term = (head_cot.astype(jnp.float32) * jax.nn.sigmoid(logits)).astype(jnp.bfloat16)
    grad = lax.psum_scatter(
        times_t(head_term, head_weight), "chan", scatter_dimension=1, tiled=True
    )
    grads = []
    for layer_number in reversed(range(conv_weight.shape[0])):
        before, whole, steps = saved[layer_number]
        grad_low = grad.astype(jnp.bfloat16)
        later = tap_grad(grad_low, -steps)
        earlier = tap_grad(grad_low, steps)
        partial_value = times_t(later, conv_weight[layer_number, 0])
        partial_value = partial_value + times_t(grad_low, conv_weight[layer_number, 1])
        partial_value = partial_value + times_t(earlier, conv_weight[layer_number, 2])
        back_u = lax.psum_scatter(partial_value, "chan", scatter_dimension=1, tiled=True)
        kernel = jnp.stack(
            [inner_rows(whole, later), inner_rows(whole, grad_low), inner_rows(whole, earlier)]
        )
        grads.append(lax.psum_scatter(kernel, "seq", scatter_dimension=1, tiled=True))
        grad = grad + activation_slope(before.astype(jnp.float32), back_u)
    kernel_gradient = jnp.stack(grads[::-1])
    resident_blocks = rows // BLOCK
    block_partial_sums = (
        tracks.astype(jnp.float32).reshape(resident_blocks, BLOCK, tracks.shape[1]).sum(axis=1)
    )
    scale = jnp.sqrt(jnp.float32(EXONS * BLOCK))
    all_blocks = lax.all_gather(block_partial_sums, "seq", axis=0, tiled=True)
    labels = jnp.arange(all_blocks.shape[0], dtype=jnp.int32)
    counts = jnp.sum((exon_blocks[:, :, None] == labels[None, None, :]).astype(jnp.float32), axis=1)
    coverage = jnp.dot(counts, all_blocks, precision=lax.Precision.HIGHEST) / scale
    return (tracks, coverage, grad.astype(jnp.bfloat16), kernel_gradient)


def solution(mesh):
    return jax.shard_map(
        shards,
        mesh=mesh,
        in_specs=(
            P("seq", "chan"),
            P(None, None, None, "chan"),
            P(None, "chan"),
            P("seq", "chan"),
            P("seq", None),
        ),
        out_specs=(
            P("seq", "chan"),
            P("seq", "chan"),
            P("seq", "chan"),
            P(None, None, "seq", "chan"),
        ),
        check_vma=False,
    )
```

profile of v0, /device:TPU:2, one launch (start us, length us, event | category | flops | bytes accessed | tf_op | source)
XLA Modules:
  0.0 468.9 jit_solution(14514463337364591084)
XLA Ops:
  7.2 2.2 fusion.30
  9.5 1.3 collective-permute-start.1
  10.8 11.8 %collective-permute-done.1 = bf16[512,384]{1,0:T(8,128)(2,1)S(1)} collective-permute-done((bf16[512,384]{1,0:T(8,128)(2,1)}, bf16[512,384]{1,0:T(8,128)(2,1)S(1)}, u32[]{:S(2)}, u32[]{:S(2)}) %collective-permute-start.1) | collective-permute-done | bytes 393248 | tf_op jit(solution)/shard_map/ppermute | solution.py:13
  23.4 3.8 collective-permute-start
  27.3 8.0 %collective-permute-done = bf16[512,384]{1,0:T(8,128)(2,1)S(1)} collective-permute-done((bf16[512,384]{1,0:T(8,128)(2,1)}, bf16[512,384]{1,0:T(8,128)(2,1)S(1)}, u32[]{:S(2)}, u32[]{:S(2)}) %collective-permute-start) | collective-permute-done | bytes 393248 | tf_op jit(solution)/shard_map/ppermute | solution.py:13
  36.1 5.5 %all-gather.9.cloned.1.call-done = bf16[512,1536]{1,0:T(8,128)(2,1)} async-done(((bf16[512,384]{1,0:T(8,128)(2,1)}), bf16[512,1536]{1,0:T(8,128)(2,1)}) %all-gather.9.cloned.1.call-update) | async-done | bytes 1572880 | tf_op jit(solution)/shard_map/all_gather | solution.py:49
  41.5 3.6 fusion.10
  45.2 27.9 %all-gather.11.cloned.1.call-done = bf16[512,1536]{1,0:T(8,128)(2,1)} async-done(((bf16[512,384]{1,0:T(8,128)(2,1)}), bf16[512,1536]{1,0:T(8,128)(2,1)}) %all-gather.11.cloned.1.call-update) | async-done | bytes 1572880 | tf_op jit(solution)/shard_map/all_gather | solution.py:51
  73.1 3.6 fusion.6
  76.7 27.4 %all-gather.7.cloned.1.call-done = bf16[512,1536]{1,0:T(8,128)(2,1)} async-done(((bf16[512,384]{1,0:T(8,128)(2,1)}), bf16[512,1536]{1,0:T(8,128)(2,1)}) %all-gather.7.cloned.1.call-update) | async-done | bytes 1572880 | tf_op jit(solution)/shard_map/all_gather | solution.py:50
  104.1 3.9 fusion.3
  108.1 29.2 %all-gather.13.cloned.1.call-done = bf16[512,1536]{1,0:T(8,128)(2,1)} async-done(((bf16[512,384]{1,0:T(8,128)(2,1)}), bf16[512,1536]{1,0:T(8,128)(2,1)}) %all-gather.13.cloned.1.call-update) | async-done | bytes 1572880 | tf_op jit(solution)/shard_map/all_gather | solution.py:59
  137.4 5.8 %convert_reduce_fusion = (f32[4,1024]{1,0:T(4,128)}, bf16[512,1024]{1,0:T(8,128)(2,1)}, f32[512,1024]{1,0:T(8,128)S(1)}) fusion(bf16[512,1536]{1,0:T(8,128)(2,1)} %all-gather.13.cloned.1.call-done, bf16[1536,1024]{1,0:T(8,128)(2,1)S(1)} %copy-done), kind=kOutput, calls=%fused_computation.8 | convolution fusion | flops 1615327232 | bytes 7880704 | tf_op jit(solution)/shard_map/dot_general | solution.py:60
  143.2 3.5 fusion.15
  147.3 40.1 %reduce-scatter.4.cloned.1.call-done = f32[512,384]{1,0:T(8,128)} async-done(((f32[512,1536]{1,0:T(8,128)}), f32[512,384]{1,0:T(8,128)}) %reduce-scatter.4.cloned.1.call-update) | async-done | bytes 786448 | tf_op jit(solution)/shard_map/reduce_scatter | solution.py:63
  187.4 1.2 convert_element_type.37
  188.6 3.7 collective-permute-start.3
  192.4 1.3 collective-permute-start.2
  193.7 2.3 fusion.8
  196.0 4.8 %collective-permute-done.3 = bf16[512,384]{1,0:T(8,128)(2,1)S(1)} collective-permute-done((bf16[512,384]{1,0:T(8,128)(2,1)S(1)}, bf16[512,384]{1,0:T(8,128)(2,1)S(1)}, u32[]{:S(2)}, u32[]{:S(2)}) %collective-permute-start.3) | collective-permute-done | bytes 393248 | tf_op jit(solution)/shard_map/ppermute | solution.py:13
  200.8 1.0 fusion.4
  201.8 3.1 collective-permute-done.2
  205.6 2.7 fusion
  208.6 2.6 convolution_bitcast_fusion.1
  211.3 1.0 convolution_bitcast_fusion
  213.3 3.3 pad_maximum_fusion
  217.4 50.6 %all-gather.15.cloned.1.call-done = f32[64,4,1024]{2,1,0:T(4,128)} async-done(((f32[1,4,1024]{2,1,0:T(4,128)}), f32[64,4,1024]{2,1,0:T(4,128)}) %all-gather.15.cloned.1.call-update) | async-done | bytes 1048592 | tf_op jit(solution)/shard_map/all_gather | solution.py:87
  268.0 2.6 reshape.20
  270.6 2.4 convolution_multiply_fusion
  273.1 34.8 %reduce-scatter.6.cloned.1.call-done = f32[512,384]{1,0:T(8,128)} async-done(((f32[512,1536]{1,0:T(8,128)}), f32[512,384]{1,0:T(8,128)}) %reduce-scatter.6.cloned.1.call-update) | async-done | bytes 786448 | tf_op jit(solution)/shard_map/reduce_scatter | solution.py:75
  307.9 2.7 fusion.26
  310.6 151.5 %reduce-scatter.8.cloned.1.call-done = f32[3,24,384]{2,1,0:T(8,128)} async-done(((f32[3,1536,384]{2,1,0:T(8,128)}), f32[3,24,384]{2,1,0:T(8,128)}) %reduce-scatter.8.cloned.1.call-update) | async-done | bytes 110608 | tf_op jit(solution)/shard_map/reduce_scatter | solution.py:79
  (44 shorter events, 5.2 us)
Async XLA Ops:
  7.2 130.2 %copy-start = (bf16[1536,1024]{1,0:T(8,128)(2,1)S(1)}, bf16[1536,1024]{1,0:T(8,128)(2,1)}, u32[]{:S(2)}) copy-start(bf16[1536,1024]{1,0:T(8,128)(2,1)} %param.7) | copy-start | bytes 9437188
  7.2 34.4 %all-gather.9.cloned.1.call-start = ((), (), s32[]{:S(2)}) async-start(), calls=%async_computation.4 | async-start | bytes 1966080 | tf_op jit(solution)/shard_map/all_gather | solution.py:49
  9.4 63.7 %all-gather.11.cloned.1.call-start = ((), (), s32[]{:S(2)}) async-start(), calls=%async_computation.5 | async-start | bytes 1966080 | tf_op jit(solution)/shard_map/all_gather | solution.py:51
  9.5 13.1 %collective-permute-start.1 = (bf16[512,384]{1,0:T(8,128)(2,1)}, bf16[512,384]{1,0:T(8,128)(2,1)S(1)}, u32[]{:S(2)}, u32[]{:S(2)}) collective-permute-start(bf16[512,384]{1,0:T(8,128)(2,1)} %fusion.30), channel_id=1, source_target_pairs={{8,0},{12,4},{16,8},{20,12},{24,16},{28,20},{32,24},{36,28},{40,32... | collective-permute-start | bytes 1179656 | tf_op jit(solution)/shard_map/ppermute | solution.py:13
  22.6 0.7 copy-start.8
  23.4 80.7 %all-gather.7.cloned.1.call-start = ((), (), s32[]{:S(2)}) async-start(), calls=%async_computation.3 | async-start | bytes 1966080 | tf_op jit(solution)/shard_map/all_gather | solution.py:50
  23.4 11.8 %collective-permute-start = (bf16[512,384]{1,0:T(8,128)(2,1)}, bf16[512,384]{1,0:T(8,128)(2,1)S(1)}, u32[]{:S(2)}, u32[]{:S(2)}) collective-permute-start(bf16[512,384]{1,0:T(8,128)(2,1)} %fusion.30), channel_id=1, source_target_pairs={{0,8},{4,12},{8,16},{12,20},{16,24},{20,28},{24,32},{28,36},{32,40... | collective-permute-start | bytes 1179656 | tf_op jit(solution)/shard_map/ppermute | solution.py:13
  35.3 0.7 copy-start.9
  36.0 101.3 %all-gather.13.cloned.1.call-start = ((), (), s32[]{:S(2)}) async-start(), calls=%async_computation.6 | async-start | bytes 1966080 | tf_op jit(solution)/shard_map/all_gather | solution.py:59
  45.2 59.0 %copy-start.2 = (bf16[512,384]{1,0:T(8,128)(2,1)S(1)}, bf16[512,384]{1,0:T(8,128)(2,1)}, u32[]{:S(2)}) copy-start(bf16[512,384]{1,0:T(8,128)(2,1)} %param.5) | copy-start | bytes 1179652
  108.1 79.3 %reduce-scatter.4.cloned.1.call-start = ((), (), s32[]{:S(2)}) async-start(), calls=%async_computation.7 | async-start | bytes 3932160 | tf_op jit(solution)/shard_map/reduce_scatter | solution.py:63
  137.4 5.8 %copy-start.12 = (bf16[512,1024]{1,0:T(8,128)(2,1)S(1)}, bf16[512,1024]{1,0:T(8,128)(2,1)}, u32[]{:S(2)}) copy-start(bf16[512,1024]{1,0:T(8,128)(2,1)} %param.8) | copy-start | bytes 3145732
  146.7 121.3 %all-gather.15.cloned.1.call-start = ((), (), s32[]{:S(2)}) async-start(), calls=%async_computation.10 | async-start | bytes 1064960 | tf_op jit(solution)/shard_map/all_gather | solution.py:87
  147.3 160.6 %reduce-scatter.6.cloned.1.call-start = ((), (), s32[]{:S(2)}) async-start(), calls=%async_computation.8 | async-start | bytes 3932160 | tf_op jit(solution)/shard_map/reduce_scatter | solution.py:75
  188.6 7.4 %copy-start.3 = (bf16[512,384]{1,0:T(8,128)(2,1)}, bf16[512,384]{1,0:T(8,128)(2,1)S(1)}, u32[]{:S(2)}) copy-start(bf16[512,384]{1,0:T(8,128)(2,1)S(1)} %convert_element_type.37) | copy-start | bytes 1179652
  188.6 12.1 %copy-start.1 = (bf16[1,3,1536,384]{3,2,1,0:T(8,128)(2,1)S(1)}, bf16[1,3,1536,384]{3,2,1,0:T(8,128)(2,1)}, u32[]{:S(2)}) copy-start(bf16[1,3,1536,384]{3,2,1,0:T(8,128)(2,1)} %param.6) | copy-start | bytes 10616836
  188.6 12.1 %collective-permute-start.3 = (bf16[512,384]{1,0:T(8,128)(2,1)S(1)}, bf16[512,384]{1,0:T(8,128)(2,1)S(1)}, u32[]{:S(2)}, u32[]{:S(2)}) collective-permute-start(bf16[512,384]{1,0:T(8,128)(2,1)S(1)} %convert_element_type.37), channel_id=1, source_target_pairs={{0,8},{4,12},{8,16},{12,20},{16,24},{20,28},{24,32},{28,36},{32,40... | collective-permute-start | bytes 1179656 | tf_op jit(solution)/shard_map/ppermute | solution.py:13
  192.4 12.5 %collective-permute-start.2 = (bf16[512,384]{1,0:T(8,128)(2,1)S(1)}, bf16[512,384]{1,0:T(8,128)(2,1)S(1)}, u32[]{:S(2)}, u32[]{:S(2)}) collective-permute-start(bf16[512,384]{1,0:T(8,128)(2,1)S(1)} %convert_element_type.37), channel_id=1, source_target_pairs={{8,0},{12,4},{16,8},{20,12},{24,16},{28,20},{32,24},{36,28},{40,32... | collective-permute-start | bytes 1179656 | tf_op jit(solution)/shard_map/ppermute | solution.py:13
  200.8 1.0 copy-start.6
  204.9 0.7 copy-start.4
  208.4 253.7 %reduce-scatter.8.cloned.1.call-start = ((), (), s32[]{:S(2)}) async-start(), calls=%async_computation.9 | async-start | bytes 7188480 | tf_op jit(solution)/shard_map/reduce_scatter | solution.py:79
  208.6 2.7 copy-start.7
  208.6 2.6 copy-start.11
  211.3 1.0 copy-start.5
  216.7 0.7 copy-start.10
Sparse Core Ops, SparseCore 0:
  10.4 31.0 all-gather.8
  44.0 29.1 all-gather.10
  75.0 29.1 all-gather.6
  108.2 29.1 all-gather.12
  146.8 40.5 reduce-scatter.3
  190.6 77.3 all-gather.14
  270.6 37.2 reduce-scatter.5
  312.7 149.2 reduce-scatter.7
where the time goes:
time: 469 us
  waiting for transfers between devices  395 us (84%)
  matrix products  33.6 us (7%)
  between operations  14.3 us (3%)
  starting transfers between devices  10.7 us (2%)
  other arithmetic  9.47 us (2%)
  local copies, waits for them, and re-layouts  5.52 us (1%)
    reduce_scatter x1, waiting for transfers between devices, shards(): lax.psum_scatter(kernel, 'seq', scatter_dimension=1, tiled=True)  151 us
    all_gather x1, waiting for transfers between devices, shards(): all_blocks = lax.all_gather(block_partial_sums, 'seq', axis=0, tiled=True)  50.6 us
    reduce_scatter x1, waiting for transfers between devices, shards(): lax.psum_scatter(times_t(head_term, head_weight), 'chan', scatter_dimensi...  40.1 us
    reduce_scatter x1, waiting for transfers between devices, shards(): lax.psum_scatter(partial_value, 'chan', scatter_dimension=1, tiled=True)  34.8 us
    all_gather x1, waiting for transfers between devices, shards(): full_state = lax.all_gather(state, 'chan', axis=1, tiled=True)  29.2 us
    all_gather x1, waiting for transfers between devices, shards(): whole_up = lax.all_gather(upper, 'chan', axis=1, tiled=True)  27.9 us
    ppermute x4, waiting for transfers between devices, shifted(): lax.ppermute(value, axis, [(source, source + steps) for source in range(l...  27.7 us
    all_gather x1, waiting for transfers between devices, shards(): whole_low = lax.all_gather(lower, 'chan', axis=1, tiled=True)  27.4 us
  transfers between devices with their start and end apart: 12, of which 12 were waited for; matrix products, arithmetic and copies ran while one was open for 6% of the time, Pallas kernels for 0%

commit v1 on v0

--- a/solution.py
+++ b/solution.py
@@ -48,7 +48,13 @@
     upper = tap_input(acted, -steps)
     whole = lax.all_gather(acted, "chan", axis=1, tiled=True)
     whole_low = lax.all_gather(lower, "chan", axis=1, tiled=True)
-    whole_up = lax.all_gather(upper, "chan", axis=1, tiled=True)
+    found = []
+    for _ in range(jax.lax.axis_size("chan")):
+        found.append(upper)
+    y = jnp.stack(found)
+    whole_up = jnp.concatenate(
+        jax.lax.all_to_all(y, axis_name="chan", split_axis=0, concat_axis=0), axis=1
+    )
     mixed = jnp.dot(whole_low, conv_weight[layer_number, 0], preferred_element_type=jnp.float32)
     mixed = mixed + jnp.dot(whole, conv_weight[layer_number, 1], preferred_element_type=jnp.float32)
     mixed = mixed + jnp.dot(

time: 469 us -> 439 us (0.936)
  waiting for transfers between devices: 395 us -> 343 us
  blocking collectives: 0 us -> 22.4 us
    all_gather x1 -> x0, waiting for transfers between devices: 27.9 us -> none  [shards(): whole_up = lax.all_gather(upper, 'chan', axis=1, tiled=True)]
    all_to_all x0 -> x1, blocking collectives: none -> 22.4 us  [shards(): jax.lax.all_to_all(y, axis_name='chan', split_axis=0, concat_axis=0)]
    all_gather x1, waiting for transfers between devices: 27.4 us -> 6.39 us  [shards(): whole_low = lax.all_gather(lower, 'chan', axis=1, tiled=True)]
    all_gather x1, waiting for transfers between devices: 5.46 us -> 0.01 us  [shards(): whole = lax.all_gather(acted, 'chan', axis=1, tiled=True)]
  transfers between devices with their start and end apart: 12 -> 11, of which waited for: 12 -> 10; matrix products, arithmetic and copies ran while one was open for 6% -> 7% of each run, Pallas kernels for 0% -> 0%
where the time goes in v1:
time: 439 us
  waiting for transfers between devices  343 us (78%)
  matrix products  33.2 us (8%)
  blocking collectives  22.4 us (5%)
  between operations  14.3 us (3%)
  starting transfers between devices  10.6 us (2%)
  other arithmetic  9.47 us (2%)
  local copies, waits for them, and re-layouts  6.07 us (1%)
    reduce_scatter x1, waiting for transfers between devices, shards(): lax.psum_scatter(kernel, 'seq', scatter_dimension=1, tiled=True)  151 us
    all_gather x1, waiting for transfers between devices, shards(): all_blocks = lax.all_gather(block_partial_sums, 'seq', axis=0, tiled=True)  50.6 us
    reduce_scatter x1, waiting for transfers between devices, shards(): lax.psum_scatter(times_t(head_term, head_weight), 'chan', scatter_dimensi...  40.1 us
    reduce_scatter x1, waiting for transfers between devices, shards(): lax.psum_scatter(partial_value, 'chan', scatter_dimension=1, tiled=True)  34.7 us
    all_gather x1, waiting for transfers between devices, shards(): full_state = lax.all_gather(state, 'chan', axis=1, tiled=True)  31.1 us
    ppermute x4, waiting for transfers between devices, shifted(): lax.ppermute(value, axis, [(source, source + steps) for source in range(l...  28.1 us
    all_to_all x1, blocking collectives, shards(): jax.lax.all_to_all(y, axis_name='chan', split_axis=0, concat_axis=0)  22.4 us
    ppermute x4, starting transfers between devices, shifted(): lax.ppermute(value, axis, [(source, source + steps) for source in range(l...  10.2 us
  transfers between devices with their start and end apart: 11, of which 10 were waited for; matrix products, arithmetic and copies ran while one was open for 7% of the time, Pallas kernels for 0%

profile of v1, /device:TPU:2, one launch (start us, length us, event | category | flops | bytes accessed | tf_op | source)
XLA Modules:
  0.0 438.8 jit_solution(9258781175730880586)
XLA Ops:
  7.2 2.2 fusion.30
  9.5 3.8 collective-permute-start
  13.3 8.6 %collective-permute-done = bf16[512,384]{1,0:T(8,128)(2,1)S(1)} collective-permute-done((bf16[512,384]{1,0:T(8,128)(2,1)}, bf16[512,384]{1,0:T(8,128)(2,1)S(1)}, u32[]{:S(2)}, u32[]{:S(2)}) %collective-permute-start) | collective-permute-done | bytes 393248 | tf_op jit(solution)/shard_map/ppermute | solution.py:13
  22.8 1.3 collective-permute-start.1
  24.1 11.5 %collective-permute-done.1 = bf16[512,384]{1,0:T(8,128)(2,1)} collective-permute-done((bf16[512,384]{1,0:T(8,128)(2,1)}, bf16[512,384]{1,0:T(8,128)(2,1)}, u32[]{:S(2)}, u32[]{:S(2)}) %collective-permute-start.1) | collective-permute-done | bytes 393248 | tf_op jit(solution)/shard_map/ppermute | solution.py:13
  35.6 1.2 copy.11
  36.9 22.4 %all_to_all.5 = bf16[4,512,384]{1,2,0:T(8,128)(2,1)S(1)} all-to-all(bf16[4,512,384]{1,2,0:T(8,128)(2,1)S(1)} %stack.22), channel_id=1, replica_groups=mesh['seq'=64,'chan'=4] {'chan'}, dimensions={0} | all-to-all | bytes 3145728 | tf_op jit(solution)/shard_map/all_to_all | solution.py:56
  59.3 3.2 fusion.6
  62.5 3.7 fusion.10
  66.2 6.4 %all-gather.6.cloned.1.call-done = bf16[512,1536]{1,0:T(8,128)(2,1)} async-done(((bf16[512,384]{1,0:T(8,128)(2,1)}), bf16[512,1536]{1,0:T(8,128)(2,1)}) %all-gather.6.cloned.1.call-update) | async-done | bytes 1572880 | tf_op jit(solution)/shard_map/all_gather | solution.py:50
  72.6 3.9 fusion.3
  76.6 31.1 %all-gather.10.cloned.1.call-done = bf16[512,1536]{1,0:T(8,128)(2,1)} async-done(((bf16[512,384]{1,0:T(8,128)(2,1)}), bf16[512,1536]{1,0:T(8,128)(2,1)}) %all-gather.10.cloned.1.call-update) | async-done | bytes 1572880 | tf_op jit(solution)/shard_map/all_gather | solution.py:65
  107.6 5.8 %convert_reduce_fusion = (f32[4,1024]{1,0:T(4,128)}, bf16[512,1024]{1,0:T(8,128)(2,1)}, f32[512,1024]{1,0:T(8,128)S(1)}) fusion(bf16[512,1536]{1,0:T(8,128)(2,1)} %all-gather.10.cloned.1.call-done, bf16[1536,1024]{1,0:T(8,128)(2,1)S(1)} %copy-done), kind=kOutput, calls=%fused_computation.8 | convolution fusion | flops 1615327232 | bytes 7880704 | tf_op jit(solution)/shard_map/dot_general | solution.py:66
  113.5 3.5 fusion.15
  117.6 40.1 %reduce-scatter.4.cloned.1.call-done = f32[512,384]{1,0:T(8,128)} async-done(((f32[512,1536]{1,0:T(8,128)}), f32[512,384]{1,0:T(8,128)}) %reduce-scatter.4.cloned.1.call-update) | async-done | bytes 786448 | tf_op jit(solution)/shard_map/reduce_scatter | solution.py:69
  157.7 1.2 convert_element_type.37
  158.9 3.8 collective-permute-start.3
  162.6 1.3 collective-permute-start.2
  163.9 2.3 fusion.8
  166.2 4.8 %collective-permute-done.3 = bf16[512,384]{1,0:T(8,128)(2,1)S(1)} collective-permute-done((bf16[512,384]{1,0:T(8,128)(2,1)S(1)}, bf16[512,384]{1,0:T(8,128)(2,1)S(1)}, u32[]{:S(2)}, u32[]{:S(2)}) %collective-permute-start.3) | collective-permute-done | bytes 393248 | tf_op jit(solution)/shard_map/ppermute | solution.py:13
  172.0 3.1 collective-permute-done.2
  175.9 2.7 fusion
  178.9 2.6 convolution_bitcast_fusion.1
  181.5 1.0 convolution_bitcast_fusion
  182.6 1.0 convolution_bitcast_fusion.2
  183.6 3.3 pad_maximum_fusion
  187.7 50.6 %all-gather.12.cloned.1.call-done = f32[64,4,1024]{2,1,0:T(4,128)} async-done(((f32[1,4,1024]{2,1,0:T(4,128)}), f32[64,4,1024]{2,1,0:T(4,128)}) %all-gather.12.cloned.1.call-update) | async-done | bytes 1048592 | tf_op jit(solution)/shard_map/all_gather | solution.py:93
  238.3 2.6 reshape.30
  240.9 2.4 convolution_multiply_fusion
  243.3 34.7 %reduce-scatter.6.cloned.1.call-done = f32[512,384]{1,0:T(8,128)} async-done(((f32[512,1536]{1,0:T(8,128)}), f32[512,384]{1,0:T(8,128)}) %reduce-scatter.6.cloned.1.call-update) | async-done | bytes 786448 | tf_op jit(solution)/shard_map/reduce_scatter | solution.py:81
  277.9 2.7 fusion.26
  280.7 151.3 %reduce-scatter.8.cloned.1.call-done = f32[3,24,384]{2,1,0:T(8,128)} async-done(((f32[3,1536,384]{2,1,0:T(8,128)}), f32[3,24,384]{2,1,0:T(8,128)}) %reduce-scatter.8.cloned.1.call-update) | async-done | bytes 110608 | tf_op jit(solution)/shard_map/reduce_scatter | solution.py:85
  (42 shorter events, 4.5 us)
Async XLA Ops:
  7.2 100.5 %copy-start = (bf16[1536,1024]{1,0:T(8,128)(2,1)S(1)}, bf16[1536,1024]{1,0:T(8,128)(2,1)}, u32[]{:S(2)}) copy-start(bf16[1536,1024]{1,0:T(8,128)(2,1)} %param.7) | copy-start | bytes 9437188
  7.2 55.3 %all-gather.8.cloned.1.call-start = ((), (), s32[]{:S(2)}) async-start(), calls=%async_computation.5 | async-start | bytes 1966080 | tf_op jit(solution)/shard_map/all_gather | solution.py:49
  9.4 63.1 %all-gather.6.cloned.1.call-start = ((), (), s32[]{:S(2)}) async-start(), calls=%async_computation.4 | async-start | bytes 1966080 | tf_op jit(solution)/shard_map/all_gather | solution.py:50
  9.5 12.5 %collective-permute-start = (bf16[512,384]{1,0:T(8,128)(2,1)}, bf16[512,384]{1,0:T(8,128)(2,1)S(1)}, u32[]{:S(2)}, u32[]{:S(2)}) collective-permute-start(bf16[512,384]{1,0:T(8,128)(2,1)} %fusion.30), channel_id=1, source_target_pairs={{0,8},{4,12},{8,16},{12,20},{16,24},{20,28},{24,32},{28,36},{32,40... | collective-permute-start | bytes 1179656 | tf_op jit(solution)/shard_map/ppermute | solution.py:13
  22.0 0.8 copy-start.8
  22.8 84.9 %all-gather.10.cloned.1.call-start = ((), (), s32[]{:S(2)}) async-start(), calls=%async_computation.6 | async-start | bytes 1966080 | tf_op jit(solution)/shard_map/all_gather | solution.py:65
  22.8 12.8 %collective-permute-start.1 = (bf16[512,384]{1,0:T(8,128)(2,1)}, bf16[512,384]{1,0:T(8,128)(2,1)}, u32[]{:S(2)}, u32[]{:S(2)}) collective-permute-start(bf16[512,384]{1,0:T(8,128)(2,1)} %fusion.30), channel_id=1, source_target_pairs={{8,0},{12,4},{16,8},{20,12},{24,16},{28,20},{32,24},{36,28},{40,32... | collective-permute-start | bytes 1179656 | tf_op jit(solution)/shard_map/ppermute | solution.py:13
  62.5 10.1 %copy-start.2 = (bf16[512,384]{1,0:T(8,128)(2,1)S(1)}, bf16[512,384]{1,0:T(8,128)(2,1)}, u32[]{:S(2)}) copy-start(bf16[512,384]{1,0:T(8,128)(2,1)} %param.5) | copy-start | bytes 1179652
  76.5 81.2 %reduce-scatter.4.cloned.1.call-start = ((), (), s32[]{:S(2)}) async-start(), calls=%async_computation.7 | async-start | bytes 3932160 | tf_op jit(solution)/shard_map/reduce_scatter | solution.py:69
  107.6 5.8 %copy-start.11 = (bf16[512,1024]{1,0:T(8,128)(2,1)S(1)}, bf16[512,1024]{1,0:T(8,128)(2,1)}, u32[]{:S(2)}) copy-start(bf16[512,1024]{1,0:T(8,128)(2,1)} %param.8) | copy-start | bytes 3145732
  117.0 121.3 %all-gather.12.cloned.1.call-start = ((), (), s32[]{:S(2)}) async-start(), calls=%async_computation.10 | async-start | bytes 1064960 | tf_op jit(solution)/shard_map/all_gather | solution.py:93
  117.6 160.4 %reduce-scatter.6.cloned.1.call-start = ((), (), s32[]{:S(2)}) async-start(), calls=%async_computation.8 | async-start | bytes 3932160 | tf_op jit(solution)/shard_map/reduce_scatter | solution.py:81
  158.8 7.4 %copy-start.3 = (bf16[512,384]{1,0:T(8,128)(2,1)}, bf16[512,384]{1,0:T(8,128)(2,1)S(1)}, u32[]{:S(2)}) copy-start(bf16[512,384]{1,0:T(8,128)(2,1)S(1)} %convert_element_type.37) | copy-start | bytes 1179652
  158.8 12.2 %copy-start.1 = (bf16[1,3,1536,384]{3,2,1,0:T(8,128)(2,1)S(1)}, bf16[1,3,1536,384]{3,2,1,0:T(8,128)(2,1)}, u32[]{:S(2)}) copy-start(bf16[1,3,1536,384]{3,2,1,0:T(8,128)(2,1)} %param.6) | copy-start | bytes 10616836
  158.9 12.1 %collective-permute-start.3 = (bf16[512,384]{1,0:T(8,128)(2,1)S(1)}, bf16[512,384]{1,0:T(8,128)(2,1)S(1)}, u32[]{:S(2)}, u32[]{:S(2)}) collective-permute-start(bf16[512,384]{1,0:T(8,128)(2,1)S(1)} %convert_element_type.37), channel_id=1, source_target_pairs={{0,8},{4,12},{8,16},{12,20},{16,24},{20,28},{24,32},{28,36},{32,40... | collective-permute-start | bytes 1179656 | tf_op jit(solution)/shard_map/ppermute | solution.py:13
  162.6 12.5 %collective-permute-start.2 = (bf16[512,384]{1,0:T(8,128)(2,1)S(1)}, bf16[512,384]{1,0:T(8,128)(2,1)S(1)}, u32[]{:S(2)}, u32[]{:S(2)}) collective-permute-start(bf16[512,384]{1,0:T(8,128)(2,1)S(1)} %convert_element_type.37), channel_id=1, source_target_pairs={{8,0},{12,4},{16,8},{20,12},{24,16},{28,20},{32,24},{36,28},{40,32... | collective-permute-start | bytes 1179656 | tf_op jit(solution)/shard_map/ppermute | solution.py:13
  171.0 1.0 copy-start.6
  175.1 0.7 copy-start.4
  178.6 253.3 %reduce-scatter.8.cloned.1.call-start = ((), (), s32[]{:S(2)}) async-start(), calls=%async_computation.9 | async-start | bytes 7188480 | tf_op jit(solution)/shard_map/reduce_scatter | solution.py:85
  178.9 2.7 copy-start.7
  178.9 2.6 copy-start.10
  181.5 1.0 copy-start.5
  186.9 0.7 copy-start.9
Sparse Core Ops, SparseCore 0:
  10.4 31.5 all-gather.7
  43.9 28.6 all-gather.5
  76.6 30.9 all-gather.9
  117.1 40.5 reduce-scatter.3
  160.9 77.3 all-gather.11
  240.7 37.2 reduce-scatter.5
  282.8 149.1 reduce-scatter.7
